TPU v7x, 32 devices: a whole 2x2x4 slice. The times are simulated.
32 devices in a mesh: section: 2 (over x), dp: 8 (over z, core), tensor: 2 (over y).
Axes of the slice: x: 2, y: 2, z: 4, core: 2. Of those that a mesh axis runs over, the one named last changes fastest.
Arguments:
- ends_in: bfloat16 [2, 2, 2048, 2048], P('section', None, ('dp', 'tensor')), may hold values from -6 to 6
- pieces: int32 [2, 2], replicated, may hold values from 0 to 1792, as said below
- w_query: bfloat16 [2, 2048, 2048], P('section', 'dp', 'tensor'), may hold values from -0.125 to 0.125
- w_keyval: bfloat16 [2, 2048, 256], P('section', ('dp', 'tensor')), may hold values from -0.125 to 0.125
- w_output: bfloat16 [2, 2048, 2048], P('section', 'tensor', 'dp'), may hold values from -1.5 to 1.5
- w_hidden: bfloat16 [2, 2048, 8192], P('section', 'dp', 'tensor'), may hold values from -0.125 to 0.125
- w_project: bfloat16 [2, 8192, 2048], P('section', 'tensor', 'dp'), may hold values from -0.0625 to 0.0625
- norm_params: bfloat16 [2, 4, 2048], P('section', None, ('dp', 'tensor')), as said below
Outputs:
- ends_out: float32 [2, 2, 2048, 2048], P('section', None, ('dp', 'tensor'))
- grad_query: float32 [2, 2048, 2048], P('section', 'dp', 'tensor')
- grad_keyval: float32 [2, 2048, 256], P('section', ('dp', 'tensor'))
- grad_output: float32 [2, 2048, 2048], P('section', 'tensor', 'dp')
- grad_hidden: float32 [2, 2048, 8192], P('section', 'dp', 'tensor')
- grad_project: float32 [2, 8192, 2048], P('section', 'tensor', 'dp')
- grad_norms: float32 [2, 3, 2048], P('section', None, ('dp', 'tensor'))
- grad_shift: float32 [2, 2048], P('section', ('dp', 'tensor'))
Inputs may be any that keep to these rules, and one draw needn't show every extreme that they name: Each sequence has 2 picture pieces of 256 positions; the j-th starts between j * (1024) and (j + 1) * 1024 - 256. `norm_params`: gains in rows 0 and 2 lie between 0.5 and 1.5.
All inputs are finite; a program needn't handle non-finite values.
Results may differ from a plain program's by a relative error of at most 0.02.
Values may be sent and summed in bfloat16 or wider, within the bound.
No kernel may reach another device: no remote copies, remote signals or barrier semaphores. Data moves between devices by JAX's collectives and lax.ppermute only.
A program may use at most 384 MiB of HBM per device.

v0:
```python
import jax
import jax.numpy as jnp
from jax import lax
from jax.sharding import PartitionSpec as P

SPAN = 256
MICRO = 2
EPSILON = 1e-05
NEGATIVE = -1000000000.0


def in_blocks(array, dim, devices):
    shape = array.shape
    blocks = array.reshape(*shape[:dim], devices, shape[dim] // devices, *shape[dim + 1 :])
    return jnp.moveaxis(blocks, dim, 0)


def sum_at_owner(array, axis, dim):
    devices = lax.axis_size(axis)
    blocks = lax.all_to_all(in_blocks(array, dim, devices), axis, 0, 0, tiled=True)
    return jnp.sum(blocks.astype(jnp.float32), axis=0)


def from_behind(block, axis, distance):
    devices = range(lax.axis_size(axis))
    route = [(i - distance, i) for i in devices if i - distance in devices]
    return lax.ppermute(block, axis, route)


def layer_norm(values, scale_row, shift_row):
    centered = values - jnp.mean(values, -1, keepdims=True)
    spread = jnp.mean(centered * centered, -1, keepdims=True)
    return centered * lax.rsqrt(spread + EPSILON) * scale_row + shift_row


def gelu_tanh(values):
    return jax.nn.gelu(values, approximate=True)


def spread_rows(values):
    return lax.all_gather(values, "tensor", axis=1, tiled=True)


def collect_rows(terms):
    return lax.psum_scatter(
        terms.astype(jnp.bfloat16), "tensor", scatter_dimension=1, tiled=True
    ).astype(jnp.float32)


def spread_grads(values):
    return lax.all_gather(values, "tensor", axis=1, tiled=True)


def collect_grads(terms):
    return lax.psum_scatter(
        terms.astype(jnp.bfloat16), "tensor", scatter_dimension=1, tiled=True
    ).astype(jnp.float32)


def allowed_keys(starts, query_start, query_rows, length):
    query_pos = query_start + jnp.arange(query_rows, dtype=jnp.int32)
    key_pos = jnp.arange(length, dtype=jnp.int32)
    causal = key_pos[None, :] <= query_pos[:, None]
    query_in = (query_pos[None, None, :] >= starts[:, :, None]) & (
        query_pos[None, None, :] < starts[:, :, None] + SPAN
    )
    key_in = (key_pos[None, None, :] >= starts[:, :, None]) & (
        key_pos[None, None, :] < starts[:, :, None] + SPAN
    )
    shared_piece = jnp.any(query_in[:, :, :, None] & key_in[:, :, None, :], axis=1)
    return causal[None] | shared_piece


def scores_of(queries, keyval_all, allowed):
    head_size = keyval_all.shape[-1] // 2
    queries_four = queries.reshape(queries.shape[0], queries.shape[1], -1, head_size)
    keys_part = keyval_all[..., :head_size]
    scores = jnp.einsum(
        "sqhd,skd->shqk", queries_four, keys_part, preferred_element_type=jnp.float32
    ) * head_size ** (-0.5)
    return (jnp.where(allowed[:, None], scores, NEGATIVE), queries_four)


def attend_forward(queries, keyval_all, allowed):
    head_size = keyval_all.shape[-1] // 2
    scores, queries_four = scores_of(queries, keyval_all, allowed)
    peak = jnp.max(scores, -1, keepdims=True)
    log_total = peak + jnp.log(jnp.sum(jnp.exp(scores - peak), -1, keepdims=True))
    probs = jnp.exp(scores - log_total).astype(jnp.bfloat16)
    values_part = keyval_all[..., head_size:]
    attended = jnp.einsum(
        "shqk,skd->sqhd", probs, values_part, preferred_element_type=jnp.float32
    ).astype(jnp.bfloat16)
    return (log_total, attended.reshape(queries.shape))


def attend_backward(queries, keyval_all, log_total, grad_attended, allowed):
    head_size = keyval_all.shape[-1] // 2
    scores, queries_four = scores_of(queries, keyval_all, allowed)
    probs = jnp.exp(scores - log_total)
    keys_part = keyval_all[..., :head_size]
    values_part = keyval_all[..., head_size:]
    grad_four = grad_attended.reshape(queries_four.shape)
    grad_probs = jnp.einsum(
        "sqhd,skd->shqk", grad_four, values_part, preferred_element_type=jnp.float32
    )
    grad_values = jnp.einsum(
        "shqk,sqhd->skd", probs.astype(jnp.bfloat16), grad_four, preferred_element_type=jnp.float32
    )
    weighted = jnp.sum(probs * grad_probs, -1, keepdims=True)
    grad_scores = (probs * (grad_probs - weighted) * head_size ** (-0.5)).astype(jnp.bfloat16)
    grad_queries = jnp.einsum(
        "shqk,skd->sqhd", grad_scores, keys_part, preferred_element_type=jnp.float32
    )
    grad_queries = grad_queries.astype(jnp.bfloat16).reshape(queries.shape)
    grad_keys = jnp.einsum(
        "shqk,sqhd->skd", grad_scores, queries_four, preferred_element_type=jnp.float32
    )
    return (grad_queries, jnp.concatenate([grad_keys, grad_values], -1))


def layer_forward(inputs, weights, allowed):
    query_mat, keyval_mat, output_mat, hidden_mat, project_mat, norm_table = weights
    normed_local = layer_norm(inputs, norm_table[0], norm_table[1]).astype(jnp.bfloat16)
    keyval_local = jnp.einsum(
        "srd,de->sre", normed_local, keyval_mat, preferred_element_type=jnp.float32
    ).astype(jnp.bfloat16)
    keyval_all = lax.all_gather(keyval_local, ("dp", "tensor"), axis=1, tiled=True)
    normed_rows = spread_rows(normed_local)
    queries = jnp.einsum(
        "sqd,de->sqe", normed_rows, query_mat, preferred_element_type=jnp.float32
    ).astype(jnp.bfloat16)
    log_total, attended = attend_forward(queries, keyval_all, allowed)
    middle = inputs + collect_rows(
        jnp.einsum("sqe,ed->sqd", attended, output_mat, preferred_element_type=jnp.float32)
    )
    mixed_local = layer_norm(middle, norm_table[2], norm_table[3]).astype(jnp.bfloat16)
    mixed_rows = spread_rows(mixed_local)
    hidden_pre = jnp.einsum(
        "sqd,df->sqf", mixed_rows, hidden_mat, preferred_element_type=jnp.float32
    )
    hidden_act = gelu_tanh(hidden_pre).astype(jnp.bfloat16)
    outputs = middle + collect_rows(
        jnp.einsum("sqf,fd->sqd", hidden_act, project_mat, preferred_element_type=jnp.float32)
    )
    saved = (
        normed_local,
        normed_rows,
        keyval_all,
        queries,
        log_total,
        attended,
        middle,
        mixed_rows,
        hidden_pre,
        hidden_act,
    )
    return (outputs, saved)


def input_backward(inputs, grad_out, weights, allowed, saved):
    query_mat, keyval_mat, output_mat, hidden_mat, project_mat, norm_table = weights
    (
        normed_local,
        normed_rows,
        keyval_all,
        queries,
        log_total,
        attended,
        middle,
        mixed_rows,
        hidden_pre,
        hidden_act,
    ) = saved
    grad_branch = spread_grads(grad_out.astype(jnp.bfloat16))
    grad_act = jnp.einsum(
        "sqd,fd->sqf", grad_branch, project_mat, preferred_element_type=jnp.float32
    )
    grad_pre = jax.vjp(gelu_tanh, hidden_pre)[1](grad_act)[0].astype(jnp.bfloat16)
    grad_mixed = collect_grads(
        jnp.einsum("sqf,df->sqd", grad_pre, hidden_mat, preferred_element_type=jnp.float32)
    )
    second_pull = jax.vjp(layer_norm, middle, norm_table[2], norm_table[3])[1]
    grad_mid_norm, grad_gain_two, grad_bias_two = second_pull(grad_mixed)
    grad_middle = grad_out + grad_mid_norm
    grad_attn_rows = spread_grads(grad_middle.astype(jnp.bfloat16))
    grad_attended = jnp.einsum(
        "sqd,ed->sqe", grad_attn_rows, output_mat, preferred_element_type=jnp.float32
    ).astype(jnp.bfloat16)
    grad_queries, keyval_terms = attend_backward(
        queries, keyval_all, log_total, grad_attended, allowed
    )
    grad_keyval = sum_at_owner(keyval_terms.astype(jnp.bfloat16), ("dp", "tensor"), 1).astype(
        jnp.bfloat16
    )
    grad_normed = collect_grads(
        jnp.einsum("sqe,de->sqd", grad_queries, query_mat, preferred_element_type=jnp.float32)
    )
    grad_normed = grad_normed + jnp.einsum(
        "sre,de->srd", grad_keyval, keyval_mat, preferred_element_type=jnp.float32
    )
    first_pull = jax.vjp(layer_norm, inputs, norm_table[0], norm_table[1])[1]
    grad_in_norm, grad_gain_one, grad_bias_one = first_pull(grad_normed)
    grad_inputs = grad_middle + grad_in_norm
    grad_table = jnp.stack([grad_gain_one, grad_bias_one, grad_gain_two, grad_bias_two])
    pairs = (
        (normed_rows, grad_queries),
        (attended, grad_attn_rows),
        (mixed_rows, grad_pre),
        (hidden_act, grad_branch),
        (normed_local, grad_keyval),
    )
    return (grad_inputs, grad_table, pairs)


def weight_products(pairs):
    grad_querymat = jnp.einsum(
        "sqd,sqe->de", pairs[0][0], pairs[0][1], preferred_element_type=jnp.float32
    )
    grad_outmat = jnp.einsum(
        "sqe,sqd->ed", pairs[1][0], pairs[1][1], preferred_element_type=jnp.float32
    )
    grad_hidmat = jnp.einsum(
        "sqd,sqf->df", pairs[2][0], pairs[2][1], preferred_element_type=jnp.float32
    )
    grad_projmat = jnp.einsum(
        "sqf,sqd->fd", pairs[3][0], pairs[3][1], preferred_element_type=jnp.float32
    )
    grad_keyvalmat = jnp.einsum(
        "srd,sre->de", pairs[4][0], pairs[4][1], preferred_element_type=jnp.float32
    )
    return (grad_querymat, grad_outmat, grad_hidmat, grad_projmat, grad_keyvalmat)


def local(ends_in, pieces, w_query, w_keyval, w_output, w_hidden, w_project, norm_params):
    section_index = lax.axis_index("section")
    per_batch = ends_in.shape[1] // MICRO
    rows_local = ends_in.shape[2]
    width = ends_in.shape[3]
    local_ends = ends_in[0].reshape(MICRO, per_batch, rows_local, width)
    starts_all = pieces.reshape(MICRO, per_batch, pieces.shape[1])
    gathered = (
        lax.all_gather(w_query, "dp", axis=1, tiled=True),
        lax.all_gather(w_output, "dp", axis=2, tiled=True),
        lax.all_gather(w_hidden, "dp", axis=1, tiled=True),
        lax.all_gather(w_project, "dp", axis=2, tiled=True),
    )
    shared = (
        lax.all_gather(w_keyval, ("dp", "tensor"), axis=1, tiled=True),
        lax.all_gather(norm_params, ("dp", "tensor"), axis=2, tiled=True),
    )
    weights = (
        gathered[0][0],
        shared[0][0],
        gathered[1][0],
        gathered[2][0],
        gathered[3][0],
        shared[1][0].astype(jnp.float32),
    )
    query_rows = rows_local * lax.axis_size("tensor")
    query_start = lax.axis_index("dp") * query_rows
    length = query_rows * lax.axis_size("dp")
    incoming = jnp.zeros((per_batch, rows_local, width), jnp.bfloat16)
    stored = []
    layer_outs = []
    saved_list = []
    for tick_now in range(MICRO + 1):
        batch_clip = jnp.clip(tick_now - section_index, 0, MICRO - 1)
        starts = lax.dynamic_index_in_dim(starts_all, batch_clip, 0, keepdims=False)
        allowed = allowed_keys(starts, query_start, query_rows, length)
        own_rows = local_ends[min(tick_now, MICRO - 1)]
        inputs_now = jnp.where(section_index == 0, own_rows, incoming)
        stored.append(inputs_now)
        outputs, saved_now = layer_forward(inputs_now.astype(jnp.float32), weights, allowed)
        layer_outs.append(outputs)
        saved_list.append(saved_now)
        if tick_now < MICRO:
            incoming = from_behind(outputs.astype(jnp.bfloat16), "section", 1)
    stored_stack = jnp.stack(stored)
    saved_stack = tuple((jnp.stack(items) for items in zip(*saved_list)))
    totals = tuple(
        (
            jnp.zeros((1,) + arr.shape, jnp.float32)
            for arr in (weights[0], weights[2], weights[3], weights[4], weights[1])
        )
    )
    table_total = jnp.zeros((1,) + weights[5].shape, jnp.float32)
    received = jnp.zeros((per_batch, rows_local, width), jnp.bfloat16)
    input_grads = []
    for tick_now in range(MICRO + 1):
        batch_index = tick_now - 1 + section_index
        valid = ((batch_index >= 0) & (batch_index < MICRO)).astype(jnp.float32)
        batch_clip = jnp.clip(batch_index, 0, MICRO - 1)
        source_tick = jnp.clip(tick_now - 1 + 2 * section_index, 0, MICRO)
        inputs_now = lax.dynamic_index_in_dim(stored_stack, source_tick, 0, keepdims=False).astype(
            jnp.float32
        )
        starts = lax.dynamic_index_in_dim(starts_all, batch_clip, 0, keepdims=False)
        allowed = allowed_keys(starts, query_start, query_rows, length)
        fed_back = local_ends[min(tick_now, MICRO - 1)]
        grad_now = jnp.where(section_index == 1, fed_back, received).astype(jnp.float32)
        saved_now = tuple(
            (lax.dynamic_index_in_dim(item, source_tick, 0, keepdims=False) for item in saved_stack)
        )
        grad_inputs, grad_table, pairs = input_backward(
            inputs_now, grad_now, weights, allowed, saved_now
        )
        input_grads.append(grad_inputs)
        table_total = table_total + grad_table[None] * valid
        if tick_now < MICRO:
            received = from_behind(grad_inputs.astype(jnp.bfloat16), "section", -1)
        products = weight_products(pairs)
        totals = tuple((total + term[None] * valid for total, term in zip(totals, products)))
    large_part = (
        lax.psum_scatter(
            totals[0].astype(jnp.bfloat16), "dp", scatter_dimension=1, tiled=True
        ).astype(jnp.float32),
        lax.psum_scatter(
            totals[1].astype(jnp.bfloat16), "dp", scatter_dimension=2, tiled=True
        ).astype(jnp.float32),
        lax.psum_scatter(
            totals[2].astype(jnp.bfloat16), "dp", scatter_dimension=1, tiled=True
        ).astype(jnp.float32),
        lax.psum_scatter(
            totals[3].astype(jnp.bfloat16), "dp", scatter_dimension=2, tiled=True
        ).astype(jnp.float32),
    )
    small_part = (
        lax.psum_scatter(totals[4], ("dp", "tensor"), scatter_dimension=1, tiled=True),
        lax.psum_scatter(table_total, ("dp", "tensor"), scatter_dimension=2, tiled=True),
    )
    norm_totals = small_part[1]
    result_rows = [
        jnp.where(section_index == 0, input_grads[index + 1], layer_outs[index + 1])
        for index in range(MICRO)
    ]
    ends_out = jnp.stack(result_rows).reshape(1, MICRO * per_batch, rows_local, width)
    return (
        ends_out,
        large_part[0],
        small_part[0],
        large_part[1],
        large_part[2],
        large_part[3],
        norm_totals[:, :3],
        norm_totals[:, 3],
    )


def solution(mesh):
    placed = (
        P("section", None, ("dp", "tensor"), None),
        P(),
        P("section", "dp", "tensor"),
        P("section", ("dp", "tensor"), None),
        P("section", "tensor", "dp"),
        P("section", "dp", "tensor"),
        P("section", "tensor", "dp"),
        P("section", None, ("dp", "tensor")),
    )
    return jax.shard_map(
        local,
        mesh=mesh,
        in_specs=placed,
        out_specs=(
            P("section", None, ("dp", "tensor"), None),
            P("section", "dp", "tensor"),
            P("section", ("dp", "tensor"), None),
            P("section", "tensor", "dp"),
            P("section", "dp", "tensor"),
            P("section", "tensor", "dp"),
            P("section", None, ("dp", "tensor")),
            P("section", ("dp", "tensor")),
        ),
        check_vma=False,
    )
```

profile of v0, /device:TPU:0, one launch (start us, length us, event | category | flops | bytes accessed | tf_op | source)
XLA Modules:
  0.0 2126.1 jit_solution(3505118352944656290)
XLA Ops:
  8.0 34.1 %all_gather.65 = bf16[1,4,2048]{2,1,0:T(4,128)(2,1)S(1)} all-gather(bf16[1,4,128]{2,1,0:T(4,128)(2,1)} %param.15), channel_id=1, replica_groups=mesh['section'=2,'dp'=8,'tensor'=2] {'dp','tensor'}, dimensions={2}, use_global_device_ids=true | all-gather | bytes 17408 | tf_op jit(solution)/shard_map/all_gather | solution.py:250
  73.4 48.8 %all-gather.31.cloned.1.call-done = bf16[1,2048,1024]{2,1,0:T(8,128)(2,1)} async-done(((bf16[1,256,1024]{2,1,0:T(8,128)(2,1)}), bf16[1,2048,1024]{2,1,0:T(8,128)(2,1)}) %all-gather.31.cloned.1.call-update) | async-done | bytes 4194320 | tf_op jit(solution)/shard_map/all_gather | solution.py:243
  125.9 35.6 %all-gather.59.cloned.1.call-done = bf16[2048,256]{1,0:T(8,128)(2,1)} async-done(((bf16[128,256]{1,0:T(8,128)(2,1)}), bf16[2048,256]{1,0:T(8,128)(2,1)}) %all-gather.59.cloned.1.call-update) | async-done | bytes 1048592 | tf_op jit(solution)/shard_map/all_gather | solution.py:128
  187.7 22.0 %all-gather.33.cloned.1.call-done = bf16[1,1024,2048]{2,1,0:T(8,128)(2,1)} async-done(((bf16[1,1024,256]{2,1,0:T(8,128)(2,1)}), bf16[1,1024,2048]{2,1,0:T(8,128)(2,1)}) %all-gather.33.cloned.1.call-update) | async-done | bytes 4194320 | tf_op jit(solution)/shard_map/all_gather | solution.py:244
  214.2 18.7 reduce-scatter.21.cloned.1.call-done
  240.3 19.7 all-gather.35.cloned.1.call-done
  260.0 152.8 %all-gather.37.cloned.1.call-done = bf16[1,2048,4096]{2,1,0:T(8,128)(2,1)} async-done(((bf16[1,256,4096]{2,1,0:T(8,128)(2,1)}), bf16[1,2048,4096]{2,1,0:T(8,128)(2,1)}) %all-gather.37.cloned.1.call-update) | async-done | bytes 16777232 | tf_op jit(solution)/shard_map/all_gather | solution.py:245
  425.4 139.2 %all-gather.25.cloned.1.call-done = bf16[1,4096,2048]{2,1,0:T(8,128)(2,1)} async-done(((bf16[1,4096,256]{2,1,0:T(8,128)(2,1)}), bf16[1,4096,2048]{2,1,0:T(8,128)(2,1)}) %all-gather.25.cloned.1.call-update) | async-done | bytes 16777232 | tf_op jit(solution)/shard_map/all_gather | solution.py:246
  640.8 36.1 %all-gather.61.cloned.1.call-done = bf16[2048,256]{1,0:T(8,128)(2,1)} async-done(((bf16[128,256]{1,0:T(8,128)(2,1)}), bf16[2048,256]{1,0:T(8,128)(2,1)}) %all-gather.61.cloned.1.call-update) | async-done | bytes 1048592 | tf_op jit(solution)/shard_map/all_gather | solution.py:128
  709.3 19.2 reduce-scatter.25.cloned.1.call-done
  734.2 21.4 %all-gather.41.cloned.1.call-done = bf16[1,256,2048]{2,1,0:T(8,128)(2,1)} async-done(((bf16[1,128,2048]{2,1,0:T(8,128)(2,1)}), bf16[1,256,2048]{2,1,0:T(8,128)(2,1)}) %all-gather.41.cloned.1.call-update) | async-done | bytes 1048592 | tf_op jit(solution)/shard_map/all_gather | solution.py:41
  777.8 20.4 reduce-scatter.27.cloned.1.call-done
  842.1 36.9 %all-gather.63.cloned.1.call-done = bf16[2048,256]{1,0:T(8,128)(2,1)} async-done(((bf16[128,256]{1,0:T(8,128)(2,1)}), bf16[2048,256]{1,0:T(8,128)(2,1)}) %all-gather.63.cloned.1.call-update) | async-done | bytes 1048592 | tf_op jit(solution)/shard_map/all_gather | solution.py:128
  909.1 19.3 reduce-scatter.29.cloned.1.call-done
  935.6 20.1 all-gather.45.cloned.1.call-done
  1158.9 20.8 all-gather.49.cloned.1.call-done
  1204.2 20.6 reduce-scatter.35.cloned.1.call-done
  1311.8 19.1 all-to-all-done.1
  1361.3 20.7 all-gather.53.cloned.1.call-done
  1607.5 30.4 %fusion.1 = bf16[1,4096,2048]{2,1,0:T(8,128)(2,1)} fusion(f32[4096,2048]{1,0:T(8,128)} %fusion.230, f32[4096,2048]{1,0:T(8,128)} %fusion.232, f32[]{:T(128)S(6)} %convert_element_type.649, f32[]{:T(128)S(6)} %convert_element_type.648, f32[]{:T(128)S(6)} %convert_element_type.647, bf16[3,1,256,4096]{3,2,1,0:T(8,128)(2,1)} %copy-done.12, s32[]{:T(128)S(6)} %min.35, ...), kind=kOutput, calls=%fused_computation.3 | convolution fusion | flops 4345298944 | bytes 87031824 | tf_op jit(solution)/shard_map/sqf,sqd->fd/dot_general | solution.py:226
  1667.6 30.1 %fusion = bf16[1,2048,4096]{2,1,0:T(8,128)(2,1)} fusion(f32[2048,4096]{1,0:T(8,128)} %fusion.355, f32[2048,4096]{1,0:T(8,128)} %fusion.357, f32[]{:T(128)S(6)} %convert_element_type.649, f32[]{:T(128)S(6)} %convert_element_type.648, f32[]{:T(128)S(6)} %convert_element_type.647, bf16[256,4096]{1,0:T(8,128)(2,1)} %fusion.88, ...), kind=kOutput, calls=%fused_computation.2 | convolution fusion | flops 4345298944 | bytes 87031824 | tf_op jit(solution)/shard_map/sqd,sqf->df/dot_general | solution.py:223
  1719.1 166.6 %reduce-scatter.53.cloned.1.call-done = bf16[1,4096,256]{2,1,0:T(8,128)(2,1)} async-done(((bf16[1,4096,2048]{2,1,0:T(8,128)(2,1)}), bf16[1,4096,256]{2,1,0:T(8,128)(2,1)}) %reduce-scatter.53.cloned.1.call-update) | async-done | bytes 2097168 | tf_op jit(solution)/shard_map/reduce_scatter | solution.py:324
  1889.6 165.0 %reduce-scatter.51.cloned.1.call-done = bf16[1,256,4096]{2,1,0:T(8,128)(2,1)} async-done(((bf16[1,2048,4096]{2,1,0:T(8,128)(2,1)}), bf16[1,256,4096]{2,1,0:T(8,128)(2,1)}) %reduce-scatter.51.cloned.1.call-update) | async-done | bytes 2097168 | tf_op jit(solution)/shard_map/reduce_scatter | solution.py:321
  2058.8 60.7 %reduce-scatter.47.cloned.1.call-done = f32[1,128,256]{2,1,0:T(8,128)} async-done(((f32[1,2048,256]{2,1,0:T(8,128)}), f32[1,128,256]{2,1,0:T(8,128)}) %reduce-scatter.47.cloned.1.call-update) | async-done | bytes 131088 | tf_op jit(solution)/shard_map/reduce_scatter | solution.py:329
  (623 shorter events, 931.2 us)
Async XLA Ops:
  7.9 65.4 %all-gather.29.cloned.1.call-start = ((), (), s32[]{:S(2)}) async-start(), calls=%async_computation.23 | async-start | bytes 1572864 | tf_op jit(solution)/shard_map/all_gather | solution.py:41
  44.9 77.2 %all-gather.31.cloned.1.call-start = ((), (), s32[]{:S(2)}) async-start(), calls=%async_computation.24 | async-start | bytes 4718592 | tf_op jit(solution)/shard_map/all_gather | solution.py:243
  45.7 115.9 %all-gather.59.cloned.1.call-start = ((), (), s32[]{:S(2)}) async-start(), calls=%async_computation.55 | async-start | bytes 1114112 | tf_op jit(solution)/shard_map/all_gather | solution.py:128
  53.1 156.6 %all-gather.33.cloned.1.call-start = ((), (), s32[]{:S(2)}) async-start(), calls=%async_computation.25 | async-start | bytes 4718592 | tf_op jit(solution)/shard_map/all_gather | solution.py:244
  53.7 179.1 %reduce-scatter.21.cloned.1.call-start = ((), (), s32[]{:S(2)}) async-start(), calls=%async_computation.26 | async-start | bytes 1572864 | tf_op jit(solution)/shard_map/reduce_scatter | solution.py:45
  238.5 174.3 %all-gather.37.cloned.1.call-start = ((), (), s32[]{:S(2)}) async-start(), calls=%async_computation.28 | async-start | bytes 18874368 | tf_op jit(solution)/shard_map/all_gather | solution.py:245
  239.3 325.3 %all-gather.25.cloned.1.call-start = ((), (), s32[]{:S(2)}) async-start(), calls=%async_computation.21 | async-start | bytes 18874368 | tf_op jit(solution)/shard_map/all_gather | solution.py:246
  240.0 356.1 %reduce-scatter.23.cloned.1.call-start = ((), (), s32[]{:S(2)}) async-start(), calls=%async_computation.29 | async-start | bytes 1572864 | tf_op jit(solution)/shard_map/reduce_scatter | solution.py:45
  615.8 112.7 %reduce-scatter.25.cloned.1.call-start = ((), (), s32[]{:S(2)}) async-start(), calls=%async_computation.31 | async-start | bytes 1572864 | tf_op jit(solution)/shard_map/reduce_scatter | solution.py:45
  734.1 64.0 %reduce-scatter.27.cloned.1.call-start = ((), (), s32[]{:S(2)}) async-start(), calls=%async_computation.33 | async-start | bytes 1572864 | tf_op jit(solution)/shard_map/reduce_scatter | solution.py:45
  817.9 110.6 %reduce-scatter.29.cloned.1.call-start = ((), (), s32[]{:S(2)}) async-start(), calls=%async_computation.35 | async-start | bytes 1572864 | tf_op jit(solution)/shard_map/reduce_scatter | solution.py:45
  935.1 87.8 %reduce-scatter.31.cloned.1.call-start = ((), (), s32[]{:S(2)}) async-start(), calls=%async_computation.37 | async-start | bytes 1572864 | tf_op jit(solution)/shard_map/reduce_scatter | solution.py:55
  1110.1 69.6 %all-gather.49.cloned.1.call-start = ((), (), s32[]{:S(2)}) async-start(), calls=%async_computation.40 | async-start | bytes 1572864 | tf_op jit(solution)/shard_map/all_gather | solution.py:51
  1158.9 65.9 %reduce-scatter.35.cloned.1.call-start = ((), (), s32[]{:S(2)}) async-start(), calls=%async_computation.41 | async-start | bytes 1572864 | tf_op jit(solution)/shard_map/reduce_scatter | solution.py:55
  1311.7 70.3 %all-gather.53.cloned.1.call-start = ((), (), s32[]{:S(2)}) async-start(), calls=%async_computation.44 | async-start | bytes 1572864 | tf_op jit(solution)/shard_map/all_gather | solution.py:51
  1361.2 65.7 %reduce-scatter.39.cloned.1.call-start = ((), (), s32[]{:S(2)}) async-start(), calls=%async_computation.45 | async-start | bytes 1572864 | tf_op jit(solution)/shard_map/reduce_scatter | solution.py:55
  1432.5 109.3 %reduce-scatter.41.cloned.1.call-start = ((), (), s32[]{:S(2)}) async-start(), calls=%async_computation.47 | async-start | bytes 1572864 | tf_op jit(solution)/shard_map/reduce_scatter | solution.py:55
  1516.6 186.1 %reduce-scatter.43.cloned.1.call-start = ((), (), s32[]{:S(2)}) async-start(), calls=%async_computation.48 | async-start | bytes 1572864 | tf_op jit(solution)/shard_map/reduce_scatter | solution.py:45
  1529.9 176.7 %reduce-scatter.55.cloned.1.call-start = ((), (), s32[]{:S(2)}) async-start(), calls=%async_computation.58 | async-start | bytes 1114112
  1554.1 154.8 %reduce-scatter.49.cloned.1.call-start = ((), (), s32[]{:S(2)}) async-start(), calls=%async_computation.51 | async-start | bytes 4718592 | tf_op jit(solution)/shard_map/reduce_scatter | solution.py:318
  1563.3 153.7 %reduce-scatter.45.cloned.1.call-start = ((), (), s32[]{:S(2)}) async-start(), calls=%async_computation.49 | async-start | bytes 4718592 | tf_op jit(solution)/shard_map/reduce_scatter | solution.py:315
  1574.8 310.9 %reduce-scatter.53.cloned.1.call-start = ((), (), s32[]{:S(2)}) async-start(), calls=%async_computation.53 | async-start | bytes 18874368 | tf_op jit(solution)/shard_map/reduce_scatter | solution.py:324
  1637.9 416.7 %reduce-scatter.51.cloned.1.call-start = ((), (), s32[]{:S(2)}) async-start(), calls=%async_computation.52 | async-start | bytes 18874368 | tf_op jit(solution)/shard_map/reduce_scatter | solution.py:321
  1697.8 421.6 %reduce-scatter.47.cloned.1.call-start = ((), (), s32[]{:S(2)}) async-start(), calls=%async_computation.50 | async-start | bytes 2228224 | tf_op jit(solution)/shard_map/reduce_scatter | solution.py:329
  (171 other events, 6035.1 us)
Sparse Core Ops, SparseCore 0:
  10.2 40.6 all-gather.26
  75.0 47.1 all-gather.30
  124.8 36.6 all-gather.58
  162.9 46.7 all-gather.32
  261.6 151.0 all-gather.36
  414.5 150.0 all-gather.24
  613.9 22.3 all-gather.38
  638.9 37.9 all-gather.60
  734.3 21.3 all-gather.40
  815.9 22.3 all-gather.42
  840.9 37.9 all-gather.62
  934.3 21.2 all-gather.44
  957.1 21.2 all-gather.56
  1110.2 27.5 reduce-scatter.32
  1230.7 21.2 all-gather.50
  1311.8 27.5 reduce-scatter.36
  1432.7 21.3 all-gather.54
  1530.0 23.4 reduce-scatter.42
  1557.0 57.3 reduce-scatter.54
  1616.8 48.9 reduce-scatter.48
  1668.8 48.1 reduce-scatter.44
  1719.3 166.3 reduce-scatter.52
  1888.0 166.6 reduce-scatter.50
  2059.4 59.9 reduce-scatter.46
  (14 shorter events, 280.7 us)
where the time goes:
time: 2130 us
  waiting for transfers between devices  1310 us (62%)
  matrix products  516 us (24%)
  other arithmetic  180 us (8%)
  local copies, waits for them, and re-layouts  46.4 us (2%)
  blocking collectives  34.1 us (2%)
  starting transfers between devices  27.5 us (1%)
    reduce_scatter x1, waiting for transfers between devices, local(): lax.psum_scatter(totals[3].astype(jnp.bfloat16), 'dp', scatter_dimension=...  167 us
    reduce_scatter x1, waiting for transfers between devices, local(): lax.psum_scatter(totals[2].astype(jnp.bfloat16), 'dp', scatter_dimension=...  165 us
    all_gather x1, waiting for transfers between devices, local(): lax.all_gather(w_hidden, 'dp', axis=1, tiled=True)  153 us
    all_gather x1, waiting for transfers between devices, local(): lax.all_gather(w_project, 'dp', axis=2, tiled=True)  139 us
    all_gather x6, waiting for transfers between devices, spread_rows(): return lax.all_gather(values, 'tensor', axis=1, tiled=True)  110 us
    all_gather x3, waiting for transfers between devices, layer_forward(): lax.all_gather(keyval_local, ('dp', 'tensor'), axis=1, tiled=True)  109 us
    reduce_scatter x6, waiting for transfers between devices, collect_rows(): lax.psum_scatter(terms.astype(jnp.bfloat16), 'tensor', scatter_dimension=...  96.2 us
    all_gather x6, waiting for transfers between devices, spread_grads(): return lax.all_gather(values, 'tensor', axis=1, tiled=True)  69.8 us
  transfers between devices with their start and end apart: 45, of which 41 were waited for; matrix products, arithmetic and copies ran while one was open for 17% of the time, Pallas kernels for 0%

commit v1 on v0

--- a/solution.py
+++ b/solution.py
@@ -7,6 +7,29 @@
 MICRO = 2
 EPSILON = 1e-05
 NEGATIVE = -1000000000.0
+
+
+def joined_along(parts, dim):
+    shape = list(parts.shape[1:])
+    shape[dim] *= parts.shape[0]
+    return jnp.moveaxis(parts, 0, dim).reshape(shape)
+
+
+def grow_blocks(value, axis):
+    size, index = (lax.axis_size(axis), lax.axis_index(axis))
+    tiles, apart = (value[None], 1)
+    while apart < size:
+        partner_block = lax.ppermute(tiles, axis, [(i, i ^ apart) for i in range(size)])
+        low = index & apart == 0
+        tiles = jnp.concatenate(
+            [jnp.where(low, tiles, partner_block), jnp.where(low, partner_block, tiles)]
+        )
+        apart *= 2
+    return tiles
+
+
+def doubled_up(x, axis, dim):
+    return joined_along(grow_blocks(x, axis), dim)
 
 
 def in_blocks(array, dim, devices):
@@ -125,7 +148,7 @@
     keyval_local = jnp.einsum(
         "srd,de->sre", normed_local, keyval_mat, preferred_element_type=jnp.float32
     ).astype(jnp.bfloat16)
-    keyval_all = lax.all_gather(keyval_local, ("dp", "tensor"), axis=1, tiled=True)
+    keyval_all = doubled_up(keyval_local, ("dp", "tensor"), 1)
     normed_rows = spread_rows(normed_local)
     queries = jnp.einsum(
         "sqd,de->sqe", normed_rows, query_mat, preferred_element_type=jnp.float32

time: 2130 us -> 2070 us (0.972)
  waiting for transfers between devices: 1310 us -> 1230 us
    ppermute x0 -> x12, waiting for transfers between devices: none -> 115 us  [grow_blocks(): lax.ppermute(tiles, axis, [(i, i ^ apart) for i in range(size)])]
    all_gather x3 -> x0, waiting for transfers between devices: 109 us -> none  [layer_forward(): lax.all_gather(keyval_local, ('dp', 'tensor'), axis=1, tiled=True)]
    all_gather x6, waiting for transfers between devices: 110 us -> 61.3 us  [spread_rows(): return lax.all_gather(values, 'tensor', axis=1, tiled=True)]
    all_gather x1, waiting for transfers between devices: 48.8 us -> 16.2 us  [local(): lax.all_gather(w_query, 'dp', axis=1, tiled=True)]
  transfers between devices with their start and end apart: 45 -> 54, of which waited for: 41 -> 47; matrix products, arithmetic and copies ran while one was open for 17% -> 18% of each run, Pallas kernels for 0% -> 0%
where the time goes in v1:
time: 2070 us; the launch traced here: 2060 us
  waiting for transfers between devices  1230 us (59%)
  matrix products  505 us (24%)
  other arithmetic  186 us (9%)
  local copies, waits for them, and re-layouts  46.5 us (2%)
  starting transfers between devices  39.4 us (2%)
  blocking collectives  34.1 us (2%)
    reduce_scatter x1, waiting for transfers between devices, local(): lax.psum_scatter(totals[3].astype(jnp.bfloat16), 'dp', scatter_dimension=...  167 us
    reduce_scatter x1, waiting for transfers between devices, local(): lax.psum_scatter(totals[2].astype(jnp.bfloat16), 'dp', scatter_dimension=...  165 us
    all_gather x1, waiting for transfers between devices, local(): lax.all_gather(w_hidden, 'dp', axis=1, tiled=True)  153 us
    all_gather x1, waiting for transfers between devices, local(): lax.all_gather(w_project, 'dp', axis=2, tiled=True)  139 us
    ppermute x12, waiting for transfers between devices, grow_blocks(): lax.ppermute(tiles, axis, [(i, i ^ apart) for i in range(size)])  115 us
    reduce_scatter x6, waiting for transfers between devices, collect_rows(): lax.psum_scatter(terms.astype(jnp.bfloat16), 'tensor', scatter_dimension=...  100 us
    all_gather x6, waiting for transfers between devices, spread_grads(): return lax.all_gather(values, 'tensor', axis=1, tiled=True)  69.5 us
    reduce_scatter x6, waiting for transfers between devices, collect_grads(): lax.psum_scatter(terms.astype(jnp.bfloat16), 'tensor', scatter_dimension=...  65.1 us
  transfers between devices with their start and end apart: 54, of which 47 were waited for; matrix products, arithmetic and copies ran while one was open for 18% of the time, Pallas kernels for 0%

profile of v1, /device:TPU:0, one launch (start us, length us, event | category | flops | bytes accessed | tf_op | source)
XLA Modules:
  0.0 2060.7 jit_solution(4006107390098840711)
XLA Ops:
  8.0 34.1 %all_gather.56 = bf16[1,4,2048]{2,1,0:T(4,128)(2,1)S(1)} all-gather(bf16[1,4,128]{2,1,0:T(4,128)(2,1)} %param.15), channel_id=1, replica_groups=mesh['section'=2,'dp'=8,'tensor'=2] {'dp','tensor'}, dimensions={2}, use_global_device_ids=true | all-gather | bytes 17408 | tf_op jit(solution)/shard_map/all_gather | solution.py:273
  74.1 37.2 %collective-permute-done.3 = bf16[8,1,128,256]{3,2,1,0:T(8,128)(2,1)} collective-permute-done((bf16[8,1,128,256]{3,2,1,0:T(8,128)(2,1)}, bf16[8,1,128,256]{3,2,1,0:T(8,128)(2,1)}, u32[]{:S(2)}, u32[]{:S(2)}) %collective-permute-start.3) | collective-permute-done | bytes 524320 | tf_op jit(solution)/shard_map/ppermute | solution.py:22
  157.5 19.6 all-gather.27.cloned.1.call-done
  181.5 18.6 reduce-scatter.21.cloned.1.call-done
  207.6 19.7 all-gather.29.cloned.1.call-done
  227.3 152.8 %all-gather.31.cloned.1.call-done = bf16[1,2048,4096]{2,1,0:T(8,128)(2,1)} async-done(((bf16[1,256,4096]{2,1,0:T(8,128)(2,1)}), bf16[1,2048,4096]{2,1,0:T(8,128)(2,1)}) %all-gather.31.cloned.1.call-update) | async-done | bytes 16777232 | tf_op jit(solution)/shard_map/all_gather | solution.py:268
  392.7 139.1 %all-gather.19.cloned.1.call-done = bf16[1,4096,2048]{2,1,0:T(8,128)(2,1)} async-done(((bf16[1,4096,256]{2,1,0:T(8,128)(2,1)}), bf16[1,4096,2048]{2,1,0:T(8,128)(2,1)}) %all-gather.19.cloned.1.call-update) | async-done | bytes 16777232 | tf_op jit(solution)/shard_map/all_gather | solution.py:269
  544.9 18.6 reduce-scatter.23.cloned.1.call-done
  602.2 21.3 %collective-permute-done.8 = bf16[8,1,128,256]{3,2,1,0:T(8,128)(2,1)} collective-permute-done((bf16[8,1,128,256]{3,2,1,0:T(8,128)(2,1)}, bf16[8,1,128,256]{3,2,1,0:T(8,128)(2,1)}, u32[]{:S(2)}, u32[]{:S(2)}) %collective-permute-start.8) | collective-permute-done | bytes 524320 | tf_op jit(solution)/shard_map/ppermute | solution.py:22
  659.6 21.2 %reduce-scatter.25.cloned.1.call-done = bf16[1,128,2048]{2,1,0:T(8,128)(2,1)} async-done(((bf16[1,256,2048]{2,1,0:T(8,128)(2,1)}), bf16[1,128,2048]{2,1,0:T(8,128)(2,1)}) %reduce-scatter.25.cloned.1.call-update) | async-done | bytes 524304 | tf_op jit(solution)/shard_map/reduce_scatter | solution.py:68
  686.6 21.4 %all-gather.35.cloned.1.call-done = bf16[1,256,2048]{2,1,0:T(8,128)(2,1)} async-done(((bf16[1,128,2048]{2,1,0:T(8,128)(2,1)}), bf16[1,256,2048]{2,1,0:T(8,128)(2,1)}) %all-gather.35.cloned.1.call-update) | async-done | bytes 1048592 | tf_op jit(solution)/shard_map/all_gather | solution.py:64
  730.2 20.4 reduce-scatter.27.cloned.1.call-done
  787.4 22.2 %collective-permute-done.13 = bf16[8,1,128,256]{3,2,1,0:T(8,128)(2,1)} collective-permute-done((bf16[8,1,128,256]{3,2,1,0:T(8,128)(2,1)}, bf16[8,1,128,256]{3,2,1,0:T(8,128)(2,1)}, u32[]{:S(2)}, u32[]{:S(2)}) %collective-permute-start.13) | collective-permute-done | bytes 524320 | tf_op jit(solution)/shard_map/ppermute | solution.py:22
  842.3 21.4 %reduce-scatter.29.cloned.1.call-done = bf16[1,128,2048]{2,1,0:T(8,128)(2,1)} async-done(((bf16[1,256,2048]{2,1,0:T(8,128)(2,1)}), bf16[1,128,2048]{2,1,0:T(8,128)(2,1)}) %reduce-scatter.29.cloned.1.call-update) | async-done | bytes 524304 | tf_op jit(solution)/shard_map/reduce_scatter | solution.py:68
  870.8 20.1 all-gather.39.cloned.1.call-done
  1094.0 20.7 %all-gather.43.cloned.1.call-done = bf16[1,256,2048]{2,1,0:T(8,128)(2,1)} async-done(((bf16[1,128,2048]{2,1,0:T(8,128)(2,1)}), bf16[1,256,2048]{2,1,0:T(8,128)(2,1)}) %all-gather.43.cloned.1.call-update) | async-done | bytes 1048592 | tf_op jit(solution)/shard_map/all_gather | solution.py:74
  1139.1 20.6 reduce-scatter.35.cloned.1.call-done
  1246.6 19.1 all-to-all-done.1
  1296.1 20.7 %all-gather.47.cloned.1.call-done = bf16[1,256,2048]{2,1,0:T(8,128)(2,1)} async-done(((bf16[1,128,2048]{2,1,0:T(8,128)(2,1)}), bf16[1,256,2048]{2,1,0:T(8,128)(2,1)}) %all-gather.47.cloned.1.call-update) | async-done | bytes 1048592 | tf_op jit(solution)/shard_map/all_gather | solution.py:74
  1542.0 30.4 %fusion.1 = bf16[1,4096,2048]{2,1,0:T(8,128)(2,1)} fusion(f32[4096,2048]{1,0:T(8,128)} %fusion.230, f32[4096,2048]{1,0:T(8,128)} %fusion.232, f32[]{:T(128)S(6)} %convert_element_type.640, f32[]{:T(128)S(6)} %convert_element_type.639, f32[]{:T(128)S(6)} %convert_element_type.638, bf16[3,1,256,4096]{3,2,1,0:T(8,128)(2,1)} %copy-done.12, s32[]{:T(128)S(6)} %min.35, ...), kind=kOutput, calls=%fused_computation.3 | convolution fusion | flops 4345298944 | bytes 87031824 | tf_op jit(solution)/shard_map/sqf,sqd->fd/dot_general | solution.py:249
  1602.1 30.1 %fusion = bf16[1,2048,4096]{2,1,0:T(8,128)(2,1)} fusion(f32[2048,4096]{1,0:T(8,128)} %fusion.358, f32[2048,4096]{1,0:T(8,128)} %fusion.360, f32[]{:T(128)S(6)} %convert_element_type.640, f32[]{:T(128)S(6)} %convert_element_type.639, f32[]{:T(128)S(6)} %convert_element_type.638, bf16[256,4096]{1,0:T(8,128)(2,1)} %fusion.88, ...), kind=kOutput, calls=%fused_computation.2 | convolution fusion | flops 4345298944 | bytes 87031824 | tf_op jit(solution)/shard_map/sqd,sqf->df/dot_general | solution.py:246
  1653.5 166.6 %reduce-scatter.53.cloned.1.call-done = bf16[1,4096,256]{2,1,0:T(8,128)(2,1)} async-done(((bf16[1,4096,2048]{2,1,0:T(8,128)(2,1)}), bf16[1,4096,256]{2,1,0:T(8,128)(2,1)}) %reduce-scatter.53.cloned.1.call-update) | async-done | bytes 2097168 | tf_op jit(solution)/shard_map/reduce_scatter | solution.py:347
  1824.1 165.2 %reduce-scatter.51.cloned.1.call-done = bf16[1,256,4096]{2,1,0:T(8,128)(2,1)} async-done(((bf16[1,2048,4096]{2,1,0:T(8,128)(2,1)}), bf16[1,256,4096]{2,1,0:T(8,128)(2,1)}) %reduce-scatter.51.cloned.1.call-update) | async-done | bytes 2097168 | tf_op jit(solution)/shard_map/reduce_scatter | solution.py:344
  1993.4 60.6 %reduce-scatter.47.cloned.1.call-done = f32[1,128,256]{2,1,0:T(8,128)} async-done(((f32[1,2048,256]{2,1,0:T(8,128)}), f32[1,128,256]{2,1,0:T(8,128)}) %reduce-scatter.47.cloned.1.call-update) | async-done | bytes 131088 | tf_op jit(solution)/shard_map/reduce_scatter | solution.py:352
  (688 shorter events, 921.6 us)
Async XLA Ops:
  7.9 104.7 %all-gather.23.cloned.1.call-start = ((), (), s32[]{:S(2)}) async-start(), calls=%async_computation.23 | async-start | bytes 1572864 | tf_op jit(solution)/shard_map/all_gather | solution.py:64
  44.9 83.9 %all-gather.25.cloned.1.call-start = ((), (), s32[]{:S(2)}) async-start(), calls=%async_computation.24 | async-start | bytes 4718592 | tf_op jit(solution)/shard_map/all_gather | solution.py:266
  45.7 131.4 %all-gather.27.cloned.1.call-start = ((), (), s32[]{:S(2)}) async-start(), calls=%async_computation.25 | async-start | bytes 4718592 | tf_op jit(solution)/shard_map/all_gather | solution.py:267
  46.2 153.9 %reduce-scatter.21.cloned.1.call-start = ((), (), s32[]{:S(2)}) async-start(), calls=%async_computation.26 | async-start | bytes 1572864 | tf_op jit(solution)/shard_map/reduce_scatter | solution.py:68
  205.8 174.3 %all-gather.31.cloned.1.call-start = ((), (), s32[]{:S(2)}) async-start(), calls=%async_computation.28 | async-start | bytes 18874368 | tf_op jit(solution)/shard_map/all_gather | solution.py:268
  206.6 325.3 %all-gather.19.cloned.1.call-start = ((), (), s32[]{:S(2)}) async-start(), calls=%async_computation.21 | async-start | bytes 18874368 | tf_op jit(solution)/shard_map/all_gather | solution.py:269
  207.3 356.1 %reduce-scatter.23.cloned.1.call-start = ((), (), s32[]{:S(2)}) async-start(), calls=%async_computation.29 | async-start | bytes 1572864 | tf_op jit(solution)/shard_map/reduce_scatter | solution.py:68
  544.8 80.9 %all-gather.33.cloned.1.call-start = ((), (), s32[]{:S(2)}) async-start(), calls=%async_computation.30 | async-start | bytes 1572864 | tf_op jit(solution)/shard_map/all_gather | solution.py:64
  588.7 92.1 %reduce-scatter.25.cloned.1.call-start = ((), (), s32[]{:S(2)}) async-start(), calls=%async_computation.31 | async-start | bytes 1572864 | tf_op jit(solution)/shard_map/reduce_scatter | solution.py:68
  730.1 80.7 %all-gather.37.cloned.1.call-start = ((), (), s32[]{:S(2)}) async-start(), calls=%async_computation.34 | async-start | bytes 1572864 | tf_op jit(solution)/shard_map/all_gather | solution.py:64
  775.2 88.5 %reduce-scatter.29.cloned.1.call-start = ((), (), s32[]{:S(2)}) async-start(), calls=%async_computation.35 | async-start | bytes 1572864 | tf_op jit(solution)/shard_map/reduce_scatter | solution.py:68
  870.3 87.9 %reduce-scatter.31.cloned.1.call-start = ((), (), s32[]{:S(2)}) async-start(), calls=%async_computation.37 | async-start | bytes 1572864 | tf_op jit(solution)/shard_map/reduce_scatter | solution.py:78
  1045.1 69.6 %all-gather.43.cloned.1.call-start = ((), (), s32[]{:S(2)}) async-start(), calls=%async_computation.40 | async-start | bytes 1572864 | tf_op jit(solution)/shard_map/all_gather | solution.py:74
  1093.9 65.8 %reduce-scatter.35.cloned.1.call-start = ((), (), s32[]{:S(2)}) async-start(), calls=%async_computation.41 | async-start | bytes 1572864 | tf_op jit(solution)/shard_map/reduce_scatter | solution.py:78
  1246.5 70.3 %all-gather.47.cloned.1.call-start = ((), (), s32[]{:S(2)}) async-start(), calls=%async_computation.44 | async-start | bytes 1572864 | tf_op jit(solution)/shard_map/all_gather | solution.py:74
  1296.0 65.6 %reduce-scatter.39.cloned.1.call-start = ((), (), s32[]{:S(2)}) async-start(), calls=%async_computation.45 | async-start | bytes 1572864 | tf_op jit(solution)/shard_map/reduce_scatter | solution.py:78
  1367.3 109.0 %reduce-scatter.41.cloned.1.call-start = ((), (), s32[]{:S(2)}) async-start(), calls=%async_computation.47 | async-start | bytes 1572864 | tf_op jit(solution)/shard_map/reduce_scatter | solution.py:78
  1451.1 186.2 %reduce-scatter.43.cloned.1.call-start = ((), (), s32[]{:S(2)}) async-start(), calls=%async_computation.48 | async-start | bytes 1572864 | tf_op jit(solution)/shard_map/reduce_scatter | solution.py:68
  1464.3 176.8 %reduce-scatter.55.cloned.1.call-start = ((), (), s32[]{:S(2)}) async-start(), calls=%async_computation.55 | async-start | bytes 1114112
  1488.6 154.8 %reduce-scatter.49.cloned.1.call-start = ((), (), s32[]{:S(2)}) async-start(), calls=%async_computation.51 | async-start | bytes 4718592 | tf_op jit(solution)/shard_map/reduce_scatter | solution.py:341
  1497.8 153.6 %reduce-scatter.45.cloned.1.call-start = ((), (), s32[]{:S(2)}) async-start(), calls=%async_computation.49 | async-start | bytes 4718592 | tf_op jit(solution)/shard_map/reduce_scatter | solution.py:338
  1509.3 310.8 %reduce-scatter.53.cloned.1.call-start = ((), (), s32[]{:S(2)}) async-start(), calls=%async_computation.53 | async-start | bytes 18874368 | tf_op jit(solution)/shard_map/reduce_scatter | solution.py:347
  1572.4 416.8 %reduce-scatter.51.cloned.1.call-start = ((), (), s32[]{:S(2)}) async-start(), calls=%async_computation.52 | async-start | bytes 18874368 | tf_op jit(solution)/shard_map/reduce_scatter | solution.py:344
  1632.3 421.7 %reduce-scatter.47.cloned.1.call-start = ((), (), s32[]{:S(2)}) async-start(), calls=%async_computation.50 | async-start | bytes 2228224 | tf_op jit(solution)/shard_map/reduce_scatter | solution.py:352
  (193 other events, 5885.7 us)
Sparse Core Ops, SparseCore 0:
  10.2 40.6 all-gather.20
  75.0 53.7 all-gather.24
  130.2 46.7 all-gather.26
  205.9 21.3 all-gather.28
  229.0 151.0 all-gather.30
  381.8 150.0 all-gather.18
  588.8 21.3 all-gather.32
  659.5 21.2 reduce-scatter.24
  686.6 21.3 all-gather.34
  775.3 21.3 all-gather.36
  869.5 21.3 all-gather.38
  892.3 21.2 all-gather.50
  964.1 21.3 all-gather.40
  1045.2 27.5 reduce-scatter.32
  1165.7 21.2 all-gather.44
  1246.7 27.5 reduce-scatter.36
  1367.4 21.3 all-gather.48
  1464.4 23.4 reduce-scatter.42
  1491.5 57.3 reduce-scatter.54
  1551.2 48.9 reduce-scatter.48
  1603.2 48.1 reduce-scatter.44
  1653.7 166.3 reduce-scatter.52
  1822.6 166.6 reduce-scatter.50
  1994.0 59.9 reduce-scatter.46
  (11 shorter events, 221.0 us)
